TPU v7x, 32 devices: a whole 2x2x4 slice. The times are simulated.
32 devices in a mesh: groups: 2 (over y), bins: 16 (over z, x, core).
Axes of the slice: x: 2, y: 2, z: 4, core: 2. Of those that a mesh axis runs over, the one named last changes fastest.
Arguments:
- snapshots: bfloat16 [256, 32, 2, 256], P(('groups', 'bins')), parts along dimension 0, may hold values from -6 to 6
- directions: float32 [64, 2, 2048], P('groups'), parts along dimension 0, may hold values from -0.7 to 0.7
- positions: float32 [2, 256], replicated, may hold values from -6 to 6
- look_counts: int32 [64], P('groups'), parts along dimension 0, may hold values from 1 to 2048, as said below
- bin_order: int32 [64], P('groups'), parts along dimension 0, may hold values from 0 to 31, as said below
Outputs:
- power_map: float32 [64, 2048], P(('groups', 'bins')), parts along dimension 0
There are 2 independent parts, one for each index of `groups`. A program takes and returns all parts, laid end to end along the dimension named above; an argument that names none is the same for every part. Nothing has to cross between parts.
Inputs may be any that keep to these rules, and one draw needn't show every extreme that they name: `look_counts`: the number of looks imaged in each bin; some bin images all 2048. `bin_order`: a permutation of the 32 bins.
All inputs are finite; a program needn't handle non-finite values.
Results may differ from a plain program's by a relative error of at most 0.0003.
Values may be sent and summed in bfloat16 or wider, within the bound.
A program may use at most 64 MiB of HBM per device.

v0:
```python
import math

import jax
import jax.numpy as jnp
from jax import lax
from jax.sharding import PartitionSpec as P

LOOK_BLK = 128


def image_bin(stacked, angles, positions, look_count, bin_id, total_bins):
    sensors = positions.shape[1]
    snap_total = stacked.shape[0]
    looks = angles.shape[1]
    products = lax.dot_general(
        stacked, stacked, (((0,), (0,)), ((), ())), preferred_element_type=jnp.float32
    )
    real_cov = (products[:sensors, :sensors] + products[sensors:, sensors:]) / snap_total
    imag_cov = (products[sensors:, :sensors] - products[:sensors, sensors:]) / snap_total
    embedded = jnp.concatenate(
        [jnp.concatenate([real_cov, -imag_cov], 1), jnp.concatenate([imag_cov, real_cov], 1)], 0
    )
    identity = jnp.eye(2 * sensors, dtype=jnp.float32)
    factor = jnp.linalg.cholesky(embedded + 0.1 * identity)
    inverse = lax.linalg.triangular_solve(factor, identity, left_side=True, lower=True)
    freq_ratio = 0.5 + (bin_id.astype(jnp.float32) + 0.5) / total_bins
    active = (look_count + LOOK_BLK - 1) // LOOK_BLK

    def one_block(block, powers):
        offset = block * LOOK_BLK
        piece = lax.dynamic_slice_in_dim(angles, offset, LOOK_BLK, 1)
        phases = (
            2.0
            * math.pi
            * freq_ratio
            * (
                positions[0][:, None] * piece[0][None, :]
                + positions[1][:, None] * piece[1][None, :]
            )
        )
        steering = jnp.concatenate([jnp.cos(phases), -jnp.sin(phases)], 0)
        whitened = jnp.dot(
            inverse, steering, precision=lax.Precision.HIGHEST, preferred_element_type=jnp.float32
        )
        quadratic = jnp.sum(whitened * whitened, 0)
        look_index = offset + jnp.arange(LOOK_BLK, dtype=jnp.int32)
        values = jnp.where(look_index < look_count, sensors / quadratic, jnp.zeros_like(quadratic))
        return lax.dynamic_update_slice_in_dim(powers, values, offset, 0)

    return lax.fori_loop(0, active, one_block, jnp.zeros((looks,), jnp.float32))


def body(snapshots, directions, positions, look_counts, bin_order):
    devices = lax.axis_size("bins")
    device = lax.axis_index("bins")
    total_bins = snapshots.shape[1]
    per_device = total_bins // devices
    sensors = snapshots.shape[3]
    bin_ids = device * per_device + jnp.arange(per_device, dtype=jnp.int32)
    turned = lax.all_to_all(snapshots, "bins", split_axis=1, concat_axis=0, tiled=True)
    snap_total = turned.shape[0]
    rows = []
    for local in range(per_device):
        bin_id = bin_ids[local]
        stacked = turned[:, local].reshape(snap_total, 2 * sensors)
        angles = lax.dynamic_index_in_dim(directions, bin_id, 0, keepdims=False)
        look_count = lax.dynamic_index_in_dim(look_counts, bin_id, 0, keepdims=False)
        rows.append(image_bin(stacked, angles, positions, look_count, bin_id, total_bins))
    powers = jnp.stack(rows, 0)
    whole = lax.all_gather(powers, "bins", axis=0, tiled=True)
    my_rows = lax.dynamic_slice_in_dim(bin_order, device * per_device, per_device)
    powers = jnp.take(whole, my_rows, axis=0)
    return powers


def solution(mesh):
    placed = (
        P(("groups", "bins"), None, None, None),
        P("groups", None, None),
        P(),
        P("groups"),
        P("groups"),
    )
    return jax.shard_map(
        body, mesh=mesh, in_specs=placed, out_specs=P(("groups", "bins"), None), check_vma=False
    )
```

profile of v0, /device:TPU:0, one launch (start us, length us, event | category | flops | bytes accessed | tf_op | source)
XLA Modules:
  0.0 408.0 jit_solution(1493512582021632135)
XLA Ops:
  0.0 1.9 copy.22
  1.9 7.4 %all-to-all-start = ((bf16[8,32,2,256]{3,0,2,1:T(8,128)(2,1)}), bf16[8,32,2,256]{3,0,2,1:T(8,128)(2,1)S(1)}, u32[]{:S(2)}, u32[]{:S(2)}) async-start(bf16[8,32,2,256]{3,0,2,1:T(8,128)(2,1)} %copy.22), calls=%async_computation | async-start | bytes 524288 | tf_op jit(solution)/shard_map/all_to_all | solution.py:60
  24.4 11.7 %cholesky.286 = f32[128,128]{1,0:T(8,128)S(1)} custom-call(f32[128,128]{1,0:T(8,128)S(1)} %cholesky.426), custom_call_target="Cholesky" | custom-call | tf_op jit(solution)/shard_map/jit(cholesky)/cholesky | solution.py:24
  36.1 9.8 %custom-call.27 = f32[1,128,128]{1,2,0:T(8,128)S(1)} custom-call(f32[1,128,128]{2,1,0:T(8,128)S(1)} %get-tuple-element.304), custom_call_target="InvertDiagBlocksLowerTriangular" | custom-call | tf_op jit(solution)/shard_map/jit(cholesky)/cholesky | solution.py:24
  47.4 12.5 %cholesky.305 = f32[128,128]{1,0:T(8,128)S(1)} custom-call(f32[128,128]{1,0:T(8,128)} %cholesky.430), custom_call_target="Cholesky" | custom-call | tf_op jit(solution)/shard_map/jit(cholesky)/cholesky | solution.py:24
  60.6 10.8 %custom-call.28 = f32[1,128,128]{1,2,0:T(8,128)S(1)} custom-call(f32[1,128,128]{2,1,0:T(8,128)} %get-tuple-element.301), custom_call_target="InvertDiagBlocksLowerTriangular" | custom-call | tf_op jit(solution)/shard_map/jit(cholesky)/cholesky | solution.py:24
  72.1 11.7 %cholesky.326 = f32[128,128]{1,0:T(8,128)S(1)} custom-call(f32[128,128]{1,0:T(8,128)S(1)} %cholesky.435), custom_call_target="Cholesky" | custom-call | tf_op jit(solution)/shard_map/jit(cholesky)/cholesky | solution.py:24
  84.5 9.8 %custom-call.29 = f32[1,128,128]{1,2,0:T(8,128)S(1)} custom-call(f32[1,128,128]{2,1,0:T(8,128)S(1)} %get-tuple-element.298), custom_call_target="InvertDiagBlocksLowerTriangular" | custom-call | tf_op jit(solution)/shard_map/jit(cholesky)/cholesky | solution.py:24
  95.0 12.1 %cholesky.343 = f32[128,128]{1,0:T(8,128)S(1)} custom-call(f32[128,128]{1,0:T(8,128)S(1)} %convolution_subtract_fusion.11), custom_call_target="Cholesky" | custom-call | tf_op jit(solution)/shard_map/jit(cholesky)/cholesky | solution.py:24
  111.1 8.1 %while.30 = (s32[]{:T(128)}, f32[512,512]{1,0:T(8,128)S(1)}, s32[4,2]{0,1:T(2,128)S(1)}, f32[4,128,128]{2,1,0:T(8,128)S(1)}, s32[]{:T(128)}) while((s32[]{:T(128)}, f32[512,512]{1,0:T(8,128)S(1)}, s32[4,2]{0,1:T(2,128)S(1)}, f32[4,128,128]{2,1,0:T(8,128)S(1)}, s32[]{:T(128)}) %tuple.125), condition=%wide.while_cond, body=%wide.while_body.sunk | while | flops 2 | bytes 131181 | solution.py:25
  119.3 39.3 %custom-call.30 = f32[4,128,128]{1,2,0:T(8,128)S(1)} custom-call(f32[4,128,128]{2,1,0:T(8,128)S(1)} %get-tuple-element.217), custom_call_target="InvertDiagBlocksLowerTriangular" | custom-call | tf_op jit(solution)/shard_map/triangular_solve/custom-call.3 | solution.py:25
  161.5 1.5 convolution_subtract_fusion.5
  164.2 22.3 %while.28 = (s32[]{:T(128)}, f32[2048]{0:T(1024)S(1)}, s32[]{:T(128)}, s32[]{:T(128)}, f32[]{:T(128)}, /*index=5*/f32[2,256]{1,0:T(2,128)S(1)}, f32[2,2048]{1,0:...) while((s32[]{:T(128)}, f32[2048]{0:T(1024)S(1)}, s32[]{:T(128)}, ...), condition=%wide.region_10.13_spmd, body=%wide.region_8.12_spmd.sunk | while | flops 403014016 | bytes 1585847 | solution.py:50
  190.6 11.7 %cholesky.358 = f32[128,128]{1,0:T(8,128)S(1)} custom-call(f32[128,128]{1,0:T(8,128)S(1)} %cholesky.439), custom_call_target="Cholesky" | custom-call | tf_op jit(solution)/shard_map/jit(cholesky)/cholesky | solution.py:24
  202.3 9.8 %custom-call.31 = f32[1,128,128]{1,2,0:T(8,128)S(1)} custom-call(f32[1,128,128]{2,1,0:T(8,128)S(1)} %get-tuple-element.314), custom_call_target="InvertDiagBlocksLowerTriangular" | custom-call | tf_op jit(solution)/shard_map/jit(cholesky)/cholesky | solution.py:24
  213.0 11.7 %cholesky.377 = f32[128,128]{1,0:T(8,128)S(1)} custom-call(f32[128,128]{1,0:T(8,128)S(1)} %cholesky.443), custom_call_target="Cholesky" | custom-call | tf_op jit(solution)/shard_map/jit(cholesky)/cholesky | solution.py:24
  224.7 10.0 %custom-call.32 = f32[1,128,128]{1,2,0:T(8,128)S(1)} custom-call(f32[1,128,128]{2,1,0:T(8,128)S(1)} %get-tuple-element.311), custom_call_target="InvertDiagBlocksLowerTriangular" | custom-call | tf_op jit(solution)/shard_map/jit(cholesky)/cholesky | solution.py:24
  235.4 11.7 %cholesky.398 = f32[128,128]{1,0:T(8,128)S(1)} custom-call(f32[128,128]{1,0:T(8,128)S(1)} %cholesky.448), custom_call_target="Cholesky" | custom-call | tf_op jit(solution)/shard_map/jit(cholesky)/cholesky | solution.py:24
  247.8 9.8 %custom-call.33 = f32[1,128,128]{1,2,0:T(8,128)S(1)} custom-call(f32[1,128,128]{2,1,0:T(8,128)S(1)} %get-tuple-element.308), custom_call_target="InvertDiagBlocksLowerTriangular" | custom-call | tf_op jit(solution)/shard_map/jit(cholesky)/cholesky | solution.py:24
  258.3 11.9 %cholesky.415 = f32[128,128]{1,0:T(8,128)S(1)} custom-call(f32[128,128]{1,0:T(8,128)S(1)} %convolution_subtract_fusion.10), custom_call_target="Cholesky" | custom-call | tf_op jit(solution)/shard_map/jit(cholesky)/cholesky | solution.py:24
  274.2 8.5 %while.31 = (s32[]{:T(128)}, f32[512,512]{1,0:T(8,128)S(1)}, s32[4,2]{0,1:T(2,128)S(1)}, f32[4,128,128]{2,1,0:T(8,128)S(1)}, s32[]{:T(128)}) while((s32[]{:T(128)}, f32[512,512]{1,0:T(8,128)S(1)}, s32[4,2]{0,1:T(2,128)S(1)}, f32[4,128,128]{2,1,0:T(8,128)S(1)}, s32[]{:T(128)}) %tuple.133), condition=%wide.while_cond.clone, body=%wide.while_body.clone.sunk | while | flops 2 | bytes 131181 | solution.py:25
  282.7 39.3 %custom-call.34 = f32[4,128,128]{1,2,0:T(8,128)S(1)} custom-call(f32[4,128,128]{2,1,0:T(8,128)S(1)} %get-tuple-element.218), custom_call_target="InvertDiagBlocksLowerTriangular" | custom-call | tf_op jit(solution)/shard_map/triangular_solve/custom-call.3 | solution.py:25
  327.0 9.5 %while.29 = (s32[]{:T(128)}, f32[2048]{0:T(1024)S(1)}, s32[]{:T(128)}, s32[]{:T(128)}, f32[]{:T(128)}, /*index=5*/f32[2,256]{1,0:T(2,128)S(1)}, f32[2,2048]{1,0:...) while((s32[]{:T(128)}, f32[2048]{0:T(1024)S(1)}, s32[]{:T(128)}, ...), condition=%wide.region_13.16_spmd, body=%wide.region_11.15_spmd.sunk | while | flops 403014016 | bytes 1585847 | solution.py:50
  336.5 68.9 %all-gather = f32[16,2,2048]{2,1,0:T(2,128)S(1)} all-gather(f32[1,2,2048]{2,1,0:T(2,128)S(1)} %maximum_bitcast_fusion), channel_id=1, replica_groups=mesh['groups'=2,'bins'=16] {'bins'}, dimensions={0}, use_global_device_ids=true | all-gather | bytes 278528 | tf_op jit(solution)/shard_map/all_gather | solution.py:70
  (191 shorter events, 81.6 us)
Async XLA Ops:
  1.9 18.4 %all-to-all-start = ((bf16[8,32,2,256]{3,0,2,1:T(8,128)(2,1)}), bf16[8,32,2,256]{3,0,2,1:T(8,128)(2,1)S(1)}, u32[]{:S(2)}, u32[]{:S(2)}) async-start(bf16[8,32,2,256]{3,0,2,1:T(8,128)(2,1)} %copy.22), calls=%async_computation | async-start | bytes 524288 | tf_op jit(solution)/shard_map/all_to_all | solution.py:60
  9.8 0.7 copy-start.11
  12.4 2.5 copy-start.10
  20.8 0.7 copy-start.4
  20.8 0.8 copy-start.5
  23.4 1.0 copy-start
  24.4 21.7 %copy-start.1 = (f32[512,512]{1,0:T(8,128)S(1)}, f32[512,512]{1,0:T(8,128)}, u32[]{:S(2)}) copy-start(f32[512,512]{1,0:T(8,128)} %copy-done) | copy-start | bytes 3145732
  163.5 0.7 copy-start.8
  187.0 0.7 copy-start.6
  187.0 0.8 copy-start.7
  189.6 1.0 copy-start.2
  190.6 21.7 %copy-start.3 = (f32[512,512]{1,0:T(8,128)S(1)}, f32[512,512]{1,0:T(8,128)}, u32[]{:S(2)}) copy-start(f32[512,512]{1,0:T(8,128)} %copy-done.2) | copy-start | bytes 3145732
  406.3 0.6 copy-start.9
where the time goes:
time: 415 us; the launch traced here: 408 us
  other arithmetic  257 us (62%)
  blocking collectives  68.9 us (17%)
  local copies, waits for them, and re-layouts  36 us (9%)
  matrix products  25.3 us (6%)
  between operations  12.5 us (3%)
  starting transfers between devices  7.36 us (2%)
    another operation x28, other arithmetic, image_bin(): factor = jnp.linalg.cholesky(embedded + 0.1 * identity)  160 us
    another operation x7, other arithmetic, image_bin(): lax.linalg.triangular_solve(factor, identity, left_side=True, lower=True)  79 us
    all_gather x1, blocking collectives, body(): whole = lax.all_gather(powers, 'bins', axis=0, tiled=True)  68.9 us
    another operation x27, local copies, waits for them, and re-layouts, image_bin(): lax.linalg.triangular_solve(factor, identity, left_side=True, lower=True)  16.5 us
    dot_general x10, matrix products, one_block(): jnp.dot(inverse, steering, precision=lax.Precision.HIGHEST, preferred_ele...  11.4 us
    another operation x14, matrix products, image_bin(): lax.linalg.triangular_solve(factor, identity, left_side=True, lower=True)  9.56 us
  transfers between devices with their start and end apart: 1, of which 0 were waited for; matrix products, arithmetic and copies ran while one was open for 1% of the time, Pallas kernels for 0%

commit v1 on v0

--- a/solution.py
+++ b/solution.py
@@ -1,11 +1,191 @@
+import functools
 import math
 
 import jax
 import jax.numpy as jnp
 from jax import lax
+from jax.experimental import pallas as pl
+from jax.experimental.pallas import tpu as pltpu
 from jax.sharding import PartitionSpec as P
 
 LOOK_BLK = 128
+LOADING = 0.1
+PIVOT = 32
+WIDE = 256
+COS_TERMS = (6.528658390045166, -25.967599868774414, 60.16762924194336, -85.45014190673828,
+             64.93911743164062, -19.73920440673828, 1.0)
+SIN_TERMS = (3.2381374835968018, -14.899847030639648, 42.02592849731445, -76.70301818847656,
+             81.60513305664062, -41.34170150756836, 6.2831854820251465)
+F32 = jnp.float32
+BF16 = jnp.bfloat16
+
+
+def mm(a, b, dims=((1,), (0,)), exact=False):
+    precision = lax.Precision.HIGHEST if exact else None
+    return lax.dot_general(a, b, (dims, ((), ())), precision=precision, preferred_element_type=F32)
+
+
+def halves(x):
+    high = x.astype(BF16)
+    return high, (x - high.astype(F32)).astype(BF16)
+
+
+def polynomial(z, terms):
+    value = z * terms[0] + terms[1]
+    for term in terms[2:]:
+        value = value * z + term
+    return value
+
+
+def invert_small(blocks):
+    n = blocks[0][0].shape[0]
+    rows = lax.broadcasted_iota(jnp.int32, (n, n), 0)
+    cols = lax.broadcasted_iota(jnp.int32, (n, n), 1)
+    one_row = lax.broadcasted_iota(jnp.int32, (1, n), 1)
+    blocks = list(blocks)
+    for k in range(n):
+        for i, (re, im) in enumerate(blocks):
+            scale = 1.0 / re[k : k + 1, k : k + 1]
+            row_re = jnp.where(one_row == k, 1.0, re[k : k + 1, :]) * scale
+            row_im = jnp.where(one_row == k, 0.0, im[k : k + 1, :]) * scale
+            col_re = re[:, k : k + 1]
+            col_im = im[:, k : k + 1]
+            rest_re = jnp.where(cols == k, 0.0, re)
+            rest_im = jnp.where(cols == k, 0.0, im)
+            next_re = rest_re - col_re * row_re + col_im * row_im
+            next_im = rest_im - col_re * row_im - col_im * row_re
+            blocks[i] = (
+                jnp.where(rows == k, row_re, next_re),
+                jnp.where(rows == k, row_im, next_im),
+            )
+    return blocks
+
+
+def put_rows(whole, rows, start):
+    stop = start + rows.shape[0]
+    pieces = [rows]
+    if start:
+        pieces.insert(0, whole[:start])
+    if stop < whole.shape[0]:
+        pieces.append(whole[stop:])
+    return jnp.concatenate(pieces, 0)
+
+
+def invert(mats):
+    n = mats[0][0].shape[0]
+    mats = list(mats)
+    for start in range(0, n, PIVOT):
+        stop = start + PIVOT
+        small = invert_small([(re[start:stop, start:stop], im[start:stop, start:stop]) for re, im in mats])
+        cols = lax.broadcasted_iota(jnp.int32, (n, n), 1)
+        inside = (cols >= start) & (cols < stop)
+        unit = lax.broadcasted_iota(jnp.int32, (PIVOT, n), 0) + start == lax.broadcasted_iota(
+            jnp.int32, (PIVOT, n), 1
+        )
+        band = inside[:PIVOT]
+        for i, (re, im) in enumerate(mats):
+            row_re = jnp.where(band, unit.astype(F32), re[start:stop])
+            row_im = jnp.where(band, 0.0, im[start:stop])
+            d_re, d_im = small[i]
+            both = jnp.concatenate([row_re, row_im], 1)
+            p = mm(d_re, both, exact=True)
+            q = mm(d_im, both, exact=True)
+            t_re = p[:, :n] - q[:, n:]
+            t_im = p[:, n:] + q[:, :n]
+            both = jnp.concatenate([t_re, t_im], 1)
+            p = mm(re[:, start:stop], both, exact=True)
+            q = mm(im[:, start:stop], both, exact=True)
+            next_re = jnp.where(inside, 0.0, re) - p[:, :n] + q[:, n:]
+            next_im = jnp.where(inside, 0.0, im) - p[:, n:] - q[:, :n]
+            mats[i] = (put_rows(next_re, t_re, start), put_rows(next_im, t_im, start))
+    return mats
+
+
+def image_kernel(per_device, total_bins, order_ref, counts_ref, snaps_ref, directions_ref, spots_ref, out_ref,
+                 solver_ref, turned_ref, spot_ref):
+    first = lax.axis_index("bins") * per_device
+    snap = snaps_ref.shape[0] // per_device
+    sensors = spots_ref.shape[0]
+    looks = out_ref.shape[1]
+    ridge = LOADING * snap
+    both = snaps_ref[...].astype(F32).reshape(snap // 8, per_device, 8, 2 * sensors)
+    diag = lax.broadcasted_iota(jnp.int32, (snap, snap), 0) == lax.broadcasted_iota(jnp.int32, (snap, snap), 1)
+    mats, fields = [], []
+    for local in range(per_device):
+        data = both[:, local].reshape(snap, 2 * sensors)
+        turned = jnp.concatenate([-data[:, sensors:], data[:, :sensors]], 1)
+        top, low = data.astype(BF16), turned.astype(BF16)
+        gram_re = mm(top, top, ((1,), (1,)))
+        gram_im = mm(low, top, ((1,), (1,)))
+        mats.append((gram_re + jnp.where(diag, ridge, 0.0), gram_im))
+        fields.append((top, low))
+        turned_ref[local] = jnp.concatenate([data, turned], 0).T.astype(BF16)
+    mats = invert(mats)
+    for local in range(per_device):
+        re, im = mats[local]
+        stacked = jnp.concatenate(fields[local], 0)
+        high, low = halves(jnp.concatenate([re, -im], 1))
+        upper = mm(high, stacked) + mm(low, stacked)
+        lower = jnp.concatenate([-upper[:, sensors:], upper[:, :sensors]], 1)
+        high, low = halves(jnp.concatenate([upper, lower], 0))
+        solver_ref[local, 0] = high
+        solver_ref[local, 1] = low
+    out_ref[...] = jnp.zeros_like(out_ref)
+    for local in range(per_device):
+        bin_id = order_ref[first + local]
+        count = counts_ref[bin_id]
+        ratio = 0.5 + (bin_id.astype(F32) + 0.5) / total_bins
+        spot_ref[0] = jnp.broadcast_to(spots_ref[:, 0:1] * ratio, (sensors, 128))
+        spot_ref[1] = jnp.broadcast_to(spots_ref[:, 1:2] * ratio, (sensors, 128))
+
+        def one_block(block, carry):
+            offset = pl.multiple_of(block * WIDE, WIDE)
+            piece = directions_ref[bin_id, :, pl.ds(offset, WIDE)]
+            x = jnp.concatenate([spot_ref[0]] * (WIDE // 128), 1)
+            y = jnp.concatenate([spot_ref[1]] * (WIDE // 128), 1)
+            turns = x * piece[0:1] + y * piece[1:2]
+            turns = turns - jnp.round(turns)
+            z = turns * turns
+            cosine = polynomial(z, COS_TERMS)
+            sine = polynomial(z, SIN_TERMS) * turns
+            steering = jnp.concatenate([cosine, -sine], 0)
+            s_high, s_low = halves(steering)
+            weights = mm(solver_ref[local, 0], s_high) + mm(solver_ref[local, 1], s_high) + mm(solver_ref[local, 0], s_low)
+            w_high, w_low = halves(weights)
+            fitted = mm(turned_ref[local], w_high) + mm(turned_ref[local], w_low)
+            left = steering - fitted
+            power = jnp.sum(left * left, 0, keepdims=True) + ridge * jnp.sum(weights * weights, 0, keepdims=True)
+            index = offset + lax.broadcasted_iota(jnp.int32, (1, WIDE), 1)
+            out_ref[local : local + 1, pl.ds(offset, WIDE)] = jnp.where(index < count, LOADING * sensors / power, 0.0)
+            return carry
+
+        lax.fori_loop(0, (count + WIDE - 1) // WIDE, one_block, 0)
+
+
+def few_snapshots(snapshots, directions, positions, look_counts, bin_order):
+    devices = lax.axis_size("bins")
+    block, total_bins, _, sensors = snapshots.shape
+    per_device = total_bins // devices
+    looks = directions.shape[2]
+    ordered = jnp.take(snapshots.reshape(block, total_bins, 2 * sensors), bin_order, axis=1)
+    ordered = ordered.transpose(1, 0, 2).reshape(devices, per_device * block, 2 * sensors)
+    arrived = lax.all_to_all(ordered, "bins", split_axis=0, concat_axis=0, tiled=True)
+    arrived = arrived.reshape(devices * per_device * block, 2 * sensors)
+    snap = devices * block
+    smem = pl.BlockSpec(memory_space=pltpu.SMEM)
+    vmem = pl.BlockSpec(memory_space=pltpu.VMEM)
+    return pl.pallas_call(
+        functools.partial(image_kernel, per_device, total_bins),
+        out_shape=jax.ShapeDtypeStruct((per_device, looks), F32),
+        in_specs=[smem, smem, vmem, vmem, vmem],
+        out_specs=vmem,
+        scratch_shapes=[
+            pltpu.VMEM((per_device, 2, 2 * snap, 2 * sensors), BF16),
+            pltpu.VMEM((per_device, 2 * sensors, 2 * snap), BF16),
+            pltpu.VMEM((2, sensors, 128), F32),
+        ],
+        compiler_params=pltpu.CompilerParams(vmem_limit_bytes=40 * 1024 * 1024),
+    )(bin_order, look_counts, arrived, directions, positions.T)
 
 
 def image_bin(stacked, angles, positions, look_count, bin_id, total_bins):
@@ -50,7 +230,7 @@
     return lax.fori_loop(0, active, one_block, jnp.zeros((looks,), jnp.float32))
 
 
-def body(snapshots, directions, positions, look_counts, bin_order):
+def many_snapshots(snapshots, directions, positions, look_counts, bin_order):
     devices = lax.axis_size("bins")
     device = lax.axis_index("bins")
     total_bins = snapshots.shape[1]
@@ -73,6 +253,12 @@
     return powers
 
 
+def body(snapshots, directions, positions, look_counts, bin_order):
+    snap_total = snapshots.shape[0] * lax.axis_size("bins")
+    form = few_snapshots if snap_total < snapshots.shape[3] else many_snapshots
+    return form(snapshots, directions, positions, look_counts, bin_order)
+
+
 def solution(mesh):
     placed = (
         P(("groups", "bins"), None, None, None),

time: 415 us -> 47.9 us (0.12); the launches traced: 408 us -> 47.6 us
  other arithmetic: 257 us -> 1.55 us
  blocking collectives: 68.9 us -> 0 us
  local copies, waits for them, and re-layouts: 36 us -> 2.54 us
  Pallas kernels: 0 us -> 26 us
  matrix products: 25.3 us -> 0 us
  between operations: 12.5 us -> 0.06 us
  waiting for transfers between devices: 0.01 us -> 9.9 us
    another operation x35 -> x0, other arithmetic: 239 us -> none  [the longest x28 160 us: image_bin(): factor = jnp.linalg.cholesky(embedded + 0.1 * identity)]
    all_gather x1 -> x0, blocking collectives: 68.9 us -> none  [body(): whole = lax.all_gather(powers, 'bins', axis=0, tiled=True)]
    pallas_call x0 -> x1, Pallas kernels: none -> 26 us  [few_snapshots(): pl.pallas_call(functools.partial(image_kernel, per_device, total_bins), o...]
    another operation x37 -> x0, local copies, waits for them, and re-layouts: 17.4 us -> none  [the longest x27 16.5 us: image_bin(): lax.linalg.triangular_solve(factor, identity, left_side=True, lower=True)]
    another operation x26 -> x0, matrix products: 13.3 us -> none  [the longest x14 9.56 us: image_bin(): lax.linalg.triangular_solve(factor, identity, left_side=True, lower=True)]
    dot_general x12 -> x0, matrix products: 12 us -> none  [the longest x10 11.4 us: one_block(): jnp.dot(inverse, steering, precision=lax.Precision.HIGHEST, preferred_ele...]
    all_to_all x1, waiting for transfers between devices: 0.01 us -> 9.9 us  [few_snapshots(): lax.all_to_all(ordered, 'bins', split_axis=0, concat_axis=0, tiled=True)]
    dynamic_update_slice x10 -> x0, other arithmetic: 7.48 us -> none  [one_block(): return lax.dynamic_update_slice_in_dim(powers, values, offset, 0)]
  transfers between devices with their start and end apart: 1 -> 1, of which waited for: 0 -> 1; matrix products, arithmetic and copies ran while one was open for 1% -> 0% of each run, Pallas kernels for 0% -> 0%
where the time goes in v1:
time: 47.9 us; the launch traced here: 47.6 us
  Pallas kernels  26 us (54%)
  waiting for transfers between devices  9.9 us (21%)
  starting transfers between devices  7.49 us (16%)
  local copies, waits for them, and re-layouts  2.54 us (5%)
  other arithmetic  1.55 us (3%)
    pallas_call x1, Pallas kernels, few_snapshots(): pl.pallas_call(functools.partial(image_kernel, per_device, total_bins), o...  26 us
    all_to_all x1, waiting for transfers between devices, few_snapshots(): lax.all_to_all(ordered, 'bins', split_axis=0, concat_axis=0, tiled=True)  9.9 us
    all_to_all x1, starting transfers between devices, few_snapshots(): lax.all_to_all(ordered, 'bins', split_axis=0, concat_axis=0, tiled=True)  7.49 us
    unnamed x10, local copies, waits for them, and re-layouts  1.97 us
    select_n x2, other arithmetic, few_snapshots(): jnp.take(snapshots.reshape(block, total_bins, 2 * sensors), bin_order, ax...  1.53 us
  transfers between devices with their start and end apart: 1, of which 1 were waited for; matrix products, arithmetic and copies ran while one was open for 0% of the time, Pallas kernels for 0%

profile of v1, /device:TPU:0, one launch (start us, length us, event | category | flops | bytes accessed | tf_op | source)
XLA Modules:
  0.0 47.6 jit_solution(12538228947234099033)
XLA Ops:
  0.0 0.0 copy-start.1
  0.0 0.7 %compare_select_fusion = s32[32]{0:T(128)S(1)} fusion(s32[32]{0:T(128)} %order_ref.1), kind=kLoop, calls=%fused_computation.3 | loop fusion | flops 96 | bytes 256 | tf_op jit(solution)/shard_map/jit(_take)/jit(_where)/select_n | solution.py:170
  0.7 0.0 copy-done.1
  0.7 1.2 %copy.8 = bf16[8,32,2,256]{3,0,2,1:T(8,128)(2,1)S(1)} copy(bf16[8,32,2,256]{3,2,1,0:T(2,128)(2,1)} %param.5) | data formatting | bytes 524288 | tf_op args[0]
  1.9 0.6 %gather_fusion = bf16[32,8,512]{2,1,0:T(8,128)(2,1)S(1)} fusion(bf16[8,32,512]{2,0,1:T(8,128)(2,1)S(1)} %bitcast.6, s32[1024]{0:T(1024)S(1)} %pad_clamp_fusion), kind=kCustom, calls=%fused_computation | custom fusion | bytes 524416 | tf_op jit(solution)/shard_map/jit(_take)/gather | solution.py:170
  2.5 0.0 copy-start
  2.5 0.8 %broadcast_select_fusion = bf16[32,8,512]{2,1,0:T(8,128)(2,1)} fusion(bf16[32,8,512]{2,1,0:T(8,128)(2,1)S(1)} %gather_fusion, pred[32]{0:T(512)(128)(4,1)S(1)} %compare_and_fusion), kind=kLoop, calls=%fused_computation.1 | loop fusion | flops 131072 | bytes 524320 | tf_op jit(solution)/shard_map/jit(_take)/select_n | solution.py:170
  3.3 0.0 copy-start.3
  3.3 7.5 %all-to-all-start = ((bf16[16,16,512]{2,1,0:T(8,128)(2,1)}), bf16[16,16,512]{2,1,0:T(8,128)(2,1)S(1)}, u32[]{:S(2)}, u32[]{:S(2)}) async-start(bf16[16,16,512]{2,1,0:T(8,128)(2,1)} %bitcast.1), calls=%async_computation | async-start | bytes 524288 | tf_op jit(solution)/shard_map/all_to_all | solution.py:172
  10.8 0.0 copy-done.3
  10.8 0.1 copy.9
  11.0 9.9 %all-to-all-done = bf16[16,16,512]{2,1,0:T(8,128)(2,1)S(1)} async-done(((bf16[16,16,512]{2,1,0:T(8,128)(2,1)}), bf16[16,16,512]{2,1,0:T(8,128)(2,1)S(1)}, u32[]{:S(2)}, u32[]{:S(2)}) %all-to-all-start) | async-done | bytes 262176 | tf_op jit(solution)/shard_map/all_to_all | solution.py:172
  20.9 0.0 copy-start.2
  20.9 0.0 copy-done
  20.9 0.7 %copy-done.2 = s32[32]{0:T(128)S(1)} copy-done((s32[32]{0:T(128)S(1)}, s32[32]{0:T(128)}, u32[]{:S(2)}) %copy-start.2) | copy-done | bytes 152
  21.5 26.0 %shard_map.55 = f32[2,2048]{1,0:T(2,128)} custom-call(s32[32]{0:T(128)S(1)} %copy-done.1, s32[32]{0:T(128)S(1)} %copy-done.2, bf16[256,512]{1,0:T(8,128)(2,1)S(1)} %bitcast.4, f32[32,2,2048]{2,1,0:T(2,128)S(1)} %copy-done, f32[256,2]{1,0:T(8,128)S(1)} %bitcast.5), custom_call_target="tpu_custom_call" | custom-call | tf_op jit(solution)/shard_map/pallas_call | solution.py:177
  (2 shorter events, 0.0 us)
Async XLA Ops:
  0.0 0.7 %copy-start.1 = (s32[32]{0:T(128)S(1)}, s32[32]{0:T(128)}, u32[]{:S(2)}) copy-start(s32[32]{0:T(128)} %order_ref.1) | copy-start | bytes 388
  2.5 18.4 %copy-start = (f32[32,2,2048]{2,1,0:T(2,128)S(1)}, f32[32,2,2048]{2,1,0:T(2,128)}, u32[]{:S(2)}) copy-start(f32[32,2,2048]{2,1,0:T(2,128)} %directions_ref.1) | copy-start | bytes 1572868
  3.3 7.5 %copy-start.3 = (f32[2,256]{1,0:T(2,128)S(1)}, f32[2,256]{1,0:T(2,128)}, u32[]{:S(2)}) copy-start(f32[2,256]{1,0:T(2,128)} %param.7) | copy-start | bytes 6148
  3.3 17.5 %all-to-all-start = ((bf16[16,16,512]{2,1,0:T(8,128)(2,1)}), bf16[16,16,512]{2,1,0:T(8,128)(2,1)S(1)}, u32[]{:S(2)}, u32[]{:S(2)}) async-start(bf16[16,16,512]{2,1,0:T(8,128)(2,1)} %bitcast.1), calls=%async_computation | async-start | bytes 524288 | tf_op jit(solution)/shard_map/all_to_all | solution.py:172
  20.9 0.7 %copy-start.2 = (s32[32]{0:T(128)S(1)}, s32[32]{0:T(128)}, u32[]{:S(2)}) copy-start(s32[32]{0:T(128)} %counts_ref.1) | copy-start | bytes 388

commit v2 on v1

--- a/solution.py
+++ b/solution.py
@@ -11,7 +11,7 @@
 LOOK_BLK = 128
 LOADING = 0.1
 PIVOT = 32
-WIDE = 256
+WIDE = 512
 COS_TERMS = (6.528658390045166, -25.967599868774414, 60.16762924194336, -85.45014190673828,
              64.93911743164062, -19.73920440673828, 1.0)
 SIN_TERMS = (3.2381374835968018, -14.899847030639648, 42.02592849731445, -76.70301818847656,
@@ -162,18 +162,73 @@
         lax.fori_loop(0, (count + WIDE - 1) // WIDE, one_block, 0)
 
 
+def exchange_kernel(devices, per_device, order_ref, snaps_ref, out_ref, send_ref, send_sem, recv_sem, own_sem):
+    me = lax.axis_index("bins")
+    barrier = pltpu.get_barrier_semaphore()
+
+    def greet(step, carry):
+        peer = lax.rem(me + step, devices)
+        pl.semaphore_signal(barrier, inc=1, device_id={"bins": peer}, device_id_type=pl.DeviceIdType.MESH)
+        return carry
+
+    lax.fori_loop(1, devices, greet, 0)
+    for owner in range(devices):
+        pieces = [snaps_ref[order_ref[owner * per_device + local]].astype(F32) for local in range(per_device)]
+        send_ref[owner] = jnp.concatenate(pieces, 0).astype(BF16)
+    own = pltpu.make_async_copy(send_ref.at[me], out_ref.at[me], own_sem)
+    own.start()
+    pl.semaphore_wait(barrier, devices - 1)
+
+    def copy(step):
+        peer = lax.rem(me + step, devices)
+        return pltpu.make_async_remote_copy(
+            src_ref=send_ref.at[peer],
+            dst_ref=out_ref.at[me],
+            send_sem=send_sem.at[step],
+            recv_sem=recv_sem.at[step],
+            device_id={"bins": peer},
+            device_id_type=pl.DeviceIdType.MESH,
+        )
+
+    def start(step, carry):
+        copy(step).start()
+        return carry
+
+    def finish(step, carry):
+        copy(step).wait()
+        return carry
+
+    lax.fori_loop(1, devices, start, 0)
+    own.wait()
+    lax.fori_loop(1, devices, finish, 0)
+
+
 def few_snapshots(snapshots, directions, positions, look_counts, bin_order):
     devices = lax.axis_size("bins")
     block, total_bins, _, sensors = snapshots.shape
     per_device = total_bins // devices
     looks = directions.shape[2]
-    ordered = jnp.take(snapshots.reshape(block, total_bins, 2 * sensors), bin_order, axis=1)
-    ordered = ordered.transpose(1, 0, 2).reshape(devices, per_device * block, 2 * sensors)
-    arrived = lax.all_to_all(ordered, "bins", split_axis=0, concat_axis=0, tiled=True)
+    by_bin = snapshots.reshape(block, total_bins, 2 * sensors).transpose(1, 0, 2)
+    smem = pl.BlockSpec(memory_space=pltpu.SMEM)
+    vmem = pl.BlockSpec(memory_space=pltpu.VMEM)
+    shape = (devices, per_device * block, 2 * sensors)
+    arrived = pl.pallas_call(
+        functools.partial(exchange_kernel, devices, per_device),
+        out_shape=jax.ShapeDtypeStruct(shape, BF16),
+        in_specs=[smem, vmem],
+        out_specs=vmem,
+        scratch_shapes=[
+            pltpu.VMEM(shape, BF16),
+            pltpu.SemaphoreType.DMA((devices,)),
+            pltpu.SemaphoreType.DMA((devices,)),
+            pltpu.SemaphoreType.DMA,
+        ],
+        compiler_params=pltpu.CompilerParams(
+            collective_id=0, has_side_effects=True, vmem_limit_bytes=16 * 1024 * 1024
+        ),
+    )(bin_order, by_bin)
     arrived = arrived.reshape(devices * per_device * block, 2 * sensors)
     snap = devices * block
-    smem = pl.BlockSpec(memory_space=pltpu.SMEM)
-    vmem = pl.BlockSpec(memory_space=pltpu.VMEM)
     return pl.pallas_call(
         functools.partial(image_kernel, per_device, total_bins),
         out_shape=jax.ShapeDtypeStruct((per_device, looks), F32),

time: 47.9 us -> 38.6 us (0.81)
  waiting for transfers between devices: 9.9 us -> 0 us
  Pallas kernels: 26 us -> 35.7 us
  starting transfers between devices: 7.49 us -> 0 us
  other arithmetic: 1.55 us -> 0 us
    pallas_call x0 -> x1, Pallas kernels: none -> 11.9 us  [few_snapshots(): pl.pallas_call(functools.partial(exchange_kernel, devices, per_device), o...]
    all_to_all x1 -> x0, waiting for transfers between devices: 9.9 us -> none  [few_snapshots(): lax.all_to_all(ordered, 'bins', split_axis=0, concat_axis=0, tiled=True)]
    all_to_all x1 -> x0, starting transfers between devices: 7.49 us -> none  [few_snapshots(): lax.all_to_all(ordered, 'bins', split_axis=0, concat_axis=0, tiled=True)]
    pallas_call x1, Pallas kernels: 26 us -> 23.9 us  [few_snapshots(): pl.pallas_call(functools.partial(image_kernel, per_device, total_bins), o...]
    select_n x2 -> x0, other arithmetic: 1.53 us -> none  [few_snapshots(): jnp.take(snapshots.reshape(block, total_bins, 2 * sensors), bin_order, ax...]
    unnamed x10, local copies, waits for them, and re-layouts: 1.97 us -> 2.66 us
    gather x1 -> x0, local copies, waits for them, and re-layouts: 0.57 us -> none  [few_snapshots(): jnp.take(snapshots.reshape(block, total_bins, 2 * sensors), bin_order, ax...]
  transfers between devices with their start and end apart: 1 -> 0, of which waited for: 1 -> 0; matrix products, arithmetic and copies ran while one was open for 0% -> 0% of each run, Pallas kernels for 0% -> 0%
where the time goes in v2:
time: 38.6 us; the launch traced here: 38.4 us
  Pallas kernels  35.7 us (92%)
  local copies, waits for them, and re-layouts  2.66 us (7%)
    pallas_call x1, Pallas kernels, few_snapshots(): pl.pallas_call(functools.partial(image_kernel, per_device, total_bins), o...  23.9 us
    pallas_call x1, Pallas kernels, few_snapshots(): pl.pallas_call(functools.partial(exchange_kernel, devices, per_device), o...  11.9 us
    unnamed x10, local copies, waits for them, and re-layouts  2.66 us

profile of v2, /device:TPU:0, one launch (start us, length us, event | category | flops | bytes accessed | tf_op | source)
XLA Modules:
  0.0 38.4 jit_solution(17348701286895856161)
XLA Ops:
  0.0 0.0 copy-start
  0.0 1.2 %copy.6 = bf16[8,32,2,256]{3,0,2,1:T(8,128)(2,1)S(1)} copy(bf16[8,32,2,256]{3,2,1,0:T(2,128)(2,1)} %param.5) | data formatting | bytes 524288 | tf_op args[0]
  1.2 0.0 copy-start.1
  1.2 0.6 %copy-done.1 = s32[32]{0:T(128)S(1)} copy-done((s32[32]{0:T(128)S(1)}, s32[32]{0:T(128)}, u32[]{:S(2)}) %copy-start.1) | copy-done | bytes 152
  1.9 0.0 copy-start.3
  1.9 11.9 %shard_map.55 = bf16[16,16,512]{2,1,0:T(8,128)(2,1)S(1)} custom-call(s32[32]{0:T(128)S(1)} %copy-done.1, bf16[32,8,512]{2,1,0:T(8,128)(2,1)S(1)} %bitcast.6), custom_call_target="tpu_custom_call" | custom-call | tf_op jit(solution)/shard_map/pallas_call | solution.py:215
  13.8 0.0 copy-done.3
  13.8 0.1 copy.7
  13.9 0.0 copy-start.2
  13.9 0.0 copy-done
  14.0 0.6 %copy-done.2 = s32[32]{0:T(128)S(1)} copy-done((s32[32]{0:T(128)S(1)}, s32[32]{0:T(128)}, u32[]{:S(2)}) %copy-start.2) | copy-done | bytes 152
  14.6 23.9 %shard_map.56 = f32[2,2048]{1,0:T(2,128)} custom-call(s32[32]{0:T(128)S(1)} %copy-done.1, s32[32]{0:T(128)S(1)} %copy-done.2, bf16[256,512]{1,0:T(8,128)(2,1)S(1)} %bitcast.5, f32[32,2,2048]{2,1,0:T(2,128)S(1)} %copy-done, f32[256,2]{1,0:T(8,128)S(1)} %bitcast.7), custom_call_target="tpu_custom_call" | custom-call | tf_op jit(solution)/shard_map/pallas_call | solution.py:232
Async XLA Ops:
  0.0 13.9 %copy-start = (f32[32,2,2048]{2,1,0:T(2,128)S(1)}, f32[32,2,2048]{2,1,0:T(2,128)}, u32[]{:S(2)}) copy-start(f32[32,2,2048]{2,1,0:T(2,128)} %directions_ref.1) | copy-start | bytes 1572868
  1.2 0.7 %copy-start.1 = (s32[32]{0:T(128)S(1)}, s32[32]{0:T(128)}, u32[]{:S(2)}) copy-start(s32[32]{0:T(128)} %order_ref.3) | copy-start | bytes 388
  1.9 11.9 %copy-start.3 = (f32[2,256]{1,0:T(2,128)S(1)}, f32[2,256]{1,0:T(2,128)}, u32[]{:S(2)}) copy-start(f32[2,256]{1,0:T(2,128)} %param.7) | copy-start | bytes 6148
  13.9 0.7 %copy-start.2 = (s32[32]{0:T(128)S(1)}, s32[32]{0:T(128)}, u32[]{:S(2)}) copy-start(s32[32]{0:T(128)} %counts_ref.1) | copy-start | bytes 388

commit v3 on v2

--- a/solution.py
+++ b/solution.py
@@ -45,11 +45,11 @@
     blocks = list(blocks)
     for k in range(n):
         for i, (re, im) in enumerate(blocks):
-            scale = 1.0 / re[k : k + 1, k : k + 1]
+            col_re = jnp.broadcast_to(re[:, k : k + 1], (n, n))
+            col_im = jnp.broadcast_to(im[:, k : k + 1], (n, n))
+            scale = 1.0 / col_re[k : k + 1, :]
             row_re = jnp.where(one_row == k, 1.0, re[k : k + 1, :]) * scale
             row_im = jnp.where(one_row == k, 0.0, im[k : k + 1, :]) * scale
-            col_re = re[:, k : k + 1]
-            col_im = im[:, k : k + 1]
             rest_re = jnp.where(cols == k, 0.0, re)
             rest_im = jnp.where(cols == k, 0.0, im)
             next_re = rest_re - col_re * row_re + col_im * row_im

time: 38.6 us -> 38.5 us (level)
  no operation moved by 1% of the time
where the time goes in v3:
time: 38.5 us; the launch traced here: 38.3 us
  Pallas kernels  35.6 us (92%)
  local copies, waits for them, and re-layouts  2.66 us (7%)
    pallas_call x1, Pallas kernels, few_snapshots(): pl.pallas_call(functools.partial(image_kernel, per_device, total_bins), o...  23.7 us
    pallas_call x1, Pallas kernels, few_snapshots(): pl.pallas_call(functools.partial(exchange_kernel, devices, per_device), o...  11.9 us
    unnamed x10, local copies, waits for them, and re-layouts  2.66 us

profile of v3, /device:TPU:0, one launch (start us, length us, event | category | flops | bytes accessed | tf_op | source)
XLA Modules:
  0.0 38.3 jit_solution(8280916142602067849)
XLA Ops:
  0.0 0.0 copy-start
  0.0 1.2 %copy.6 = bf16[8,32,2,256]{3,0,2,1:T(8,128)(2,1)S(1)} copy(bf16[8,32,2,256]{3,2,1,0:T(2,128)(2,1)} %param.5) | data formatting | bytes 524288 | tf_op args[0]
  1.2 0.0 copy-start.1
  1.2 0.6 %copy-done.1 = s32[32]{0:T(128)S(1)} copy-done((s32[32]{0:T(128)S(1)}, s32[32]{0:T(128)}, u32[]{:S(2)}) %copy-start.1) | copy-done | bytes 152
  1.9 0.0 copy-start.3
  1.9 11.9 %shard_map.55 = bf16[16,16,512]{2,1,0:T(8,128)(2,1)S(1)} custom-call(s32[32]{0:T(128)S(1)} %copy-done.1, bf16[32,8,512]{2,1,0:T(8,128)(2,1)S(1)} %bitcast.6), custom_call_target="tpu_custom_call" | custom-call | tf_op jit(solution)/shard_map/pallas_call | solution.py:215
  13.8 0.0 copy-done.3
  13.8 0.1 copy.7
  13.9 0.0 copy-start.2
  13.9 0.0 copy-done
  14.0 0.6 %copy-done.2 = s32[32]{0:T(128)S(1)} copy-done((s32[32]{0:T(128)S(1)}, s32[32]{0:T(128)}, u32[]{:S(2)}) %copy-start.2) | copy-done | bytes 152
  14.6 23.7 %shard_map.56 = f32[2,2048]{1,0:T(2,128)} custom-call(s32[32]{0:T(128)S(1)} %copy-done.1, s32[32]{0:T(128)S(1)} %copy-done.2, bf16[256,512]{1,0:T(8,128)(2,1)S(1)} %bitcast.5, f32[32,2,2048]{2,1,0:T(2,128)S(1)} %copy-done, f32[256,2]{1,0:T(8,128)S(1)} %bitcast.7), custom_call_target="tpu_custom_call" | custom-call | tf_op jit(solution)/shard_map/pallas_call | solution.py:232
Async XLA Ops:
  0.0 13.9 %copy-start = (f32[32,2,2048]{2,1,0:T(2,128)S(1)}, f32[32,2,2048]{2,1,0:T(2,128)}, u32[]{:S(2)}) copy-start(f32[32,2,2048]{2,1,0:T(2,128)} %directions_ref.1) | copy-start | bytes 1572868
  1.2 0.7 %copy-start.1 = (s32[32]{0:T(128)S(1)}, s32[32]{0:T(128)}, u32[]{:S(2)}) copy-start(s32[32]{0:T(128)} %order_ref.3) | copy-start | bytes 388
  1.9 11.9 %copy-start.3 = (f32[2,256]{1,0:T(2,128)S(1)}, f32[2,256]{1,0:T(2,128)}, u32[]{:S(2)}) copy-start(f32[2,256]{1,0:T(2,128)} %param.7) | copy-start | bytes 6148
  13.9 0.7 %copy-start.2 = (s32[32]{0:T(128)S(1)}, s32[32]{0:T(128)}, u32[]{:S(2)}) copy-start(s32[32]{0:T(128)} %counts_ref.1) | copy-start | bytes 388

commit v4 on v3

--- a/solution.py
+++ b/solution.py
@@ -10,7 +10,7 @@
 
 LOOK_BLK = 128
 LOADING = 0.1
-PIVOT = 32
+PIVOT = 64
 WIDE = 512
 COS_TERMS = (6.528658390045166, -25.967599868774414, 60.16762924194336, -85.45014190673828,
              64.93911743164062, -19.73920440673828, 1.0)

time: 38.5 us -> 38 us (0.987)
  Pallas kernels: 35.6 us -> 35.2 us
    pallas_call x1, Pallas kernels: 23.7 us -> 23.3 us  [few_snapshots(): pl.pallas_call(functools.partial(image_kernel, per_device, total_bins), o...]
where the time goes in v4:
time: 38 us; the launch traced here: 37.9 us
  Pallas kernels  35.2 us (93%)
  local copies, waits for them, and re-layouts  2.66 us (7%)
    pallas_call x1, Pallas kernels, few_snapshots(): pl.pallas_call(functools.partial(image_kernel, per_device, total_bins), o...  23.3 us
    pallas_call x1, Pallas kernels, few_snapshots(): pl.pallas_call(functools.partial(exchange_kernel, devices, per_device), o...  11.9 us
    unnamed x10, local copies, waits for them, and re-layouts  2.66 us

profile of v4, /device:TPU:0, one launch (start us, length us, event | category | flops | bytes accessed | tf_op | source)
XLA Modules:
  0.0 37.9 jit_solution(18056227647204508574)
XLA Ops:
  0.0 0.0 copy-start
  0.0 1.2 %copy.6 = bf16[8,32,2,256]{3,0,2,1:T(8,128)(2,1)S(1)} copy(bf16[8,32,2,256]{3,2,1,0:T(2,128)(2,1)} %param.5) | data formatting | bytes 524288 | tf_op args[0]
  1.2 0.0 copy-start.1
  1.2 0.6 %copy-done.1 = s32[32]{0:T(128)S(1)} copy-done((s32[32]{0:T(128)S(1)}, s32[32]{0:T(128)}, u32[]{:S(2)}) %copy-start.1) | copy-done | bytes 152
  1.9 0.0 copy-start.3
  1.9 11.9 %shard_map.55 = bf16[16,16,512]{2,1,0:T(8,128)(2,1)S(1)} custom-call(s32[32]{0:T(128)S(1)} %copy-done.1, bf16[32,8,512]{2,1,0:T(8,128)(2,1)S(1)} %bitcast.6), custom_call_target="tpu_custom_call" | custom-call | tf_op jit(solution)/shard_map/pallas_call | solution.py:215
  13.8 0.0 copy-done.3
  13.8 0.1 copy.7
  13.9 0.0 copy-start.2
  13.9 0.0 copy-done
  14.0 0.6 %copy-done.2 = s32[32]{0:T(128)S(1)} copy-done((s32[32]{0:T(128)S(1)}, s32[32]{0:T(128)}, u32[]{:S(2)}) %copy-start.2) | copy-done | bytes 152
  14.6 23.3 %shard_map.56 = f32[2,2048]{1,0:T(2,128)} custom-call(s32[32]{0:T(128)S(1)} %copy-done.1, s32[32]{0:T(128)S(1)} %copy-done.2, bf16[256,512]{1,0:T(8,128)(2,1)S(1)} %bitcast.5, f32[32,2,2048]{2,1,0:T(2,128)S(1)} %copy-done, f32[256,2]{1,0:T(8,128)S(1)} %bitcast.7), custom_call_target="tpu_custom_call" | custom-call | tf_op jit(solution)/shard_map/pallas_call | solution.py:232
Async XLA Ops:
  0.0 13.9 %copy-start = (f32[32,2,2048]{2,1,0:T(2,128)S(1)}, f32[32,2,2048]{2,1,0:T(2,128)}, u32[]{:S(2)}) copy-start(f32[32,2,2048]{2,1,0:T(2,128)} %directions_ref.1) | copy-start | bytes 1572868
  1.2 0.7 %copy-start.1 = (s32[32]{0:T(128)S(1)}, s32[32]{0:T(128)}, u32[]{:S(2)}) copy-start(s32[32]{0:T(128)} %order_ref.3) | copy-start | bytes 388
  1.9 11.9 %copy-start.3 = (f32[2,256]{1,0:T(2,128)S(1)}, f32[2,256]{1,0:T(2,128)}, u32[]{:S(2)}) copy-start(f32[2,256]{1,0:T(2,128)} %param.7) | copy-start | bytes 6148
  13.9 0.7 %copy-start.2 = (s32[32]{0:T(128)S(1)}, s32[32]{0:T(128)}, u32[]{:S(2)}) copy-start(s32[32]{0:T(128)} %counts_ref.1) | copy-start | bytes 388

commit v5 on v4

--- a/solution.py
+++ b/solution.py
@@ -43,20 +43,31 @@
     cols = lax.broadcasted_iota(jnp.int32, (n, n), 1)
     one_row = lax.broadcasted_iota(jnp.int32, (1, n), 1)
     blocks = list(blocks)
-    for k in range(n):
+    for k in range(0, n, 2):
+        pair = (cols == k) | (cols == k + 1)
         for i, (re, im) in enumerate(blocks):
-            col_re = jnp.broadcast_to(re[:, k : k + 1], (n, n))
-            col_im = jnp.broadcast_to(im[:, k : k + 1], (n, n))
-            scale = 1.0 / col_re[k : k + 1, :]
-            row_re = jnp.where(one_row == k, 1.0, re[k : k + 1, :]) * scale
-            row_im = jnp.where(one_row == k, 0.0, im[k : k + 1, :]) * scale
-            rest_re = jnp.where(cols == k, 0.0, re)
-            rest_im = jnp.where(cols == k, 0.0, im)
-            next_re = rest_re - col_re * row_re + col_im * row_im
-            next_im = rest_im - col_re * row_im - col_im * row_re
+            c0_re = jnp.broadcast_to(re[:, k : k + 1], (n, n))
+            c0_im = jnp.broadcast_to(im[:, k : k + 1], (n, n))
+            c1_re = jnp.broadcast_to(re[:, k + 1 : k + 2], (n, n))
+            c1_im = jnp.broadcast_to(im[:, k + 1 : k + 2], (n, n))
+            a, c = c0_re[k : k + 1], c1_re[k + 1 : k + 2]
+            b_re, b_im = c1_re[k : k + 1], c1_im[k : k + 1]
+            scale = 1.0 / (a * c - (b_re * b_re + b_im * b_im))
+            a, c, b_re, b_im = a * scale, c * scale, b_re * scale, b_im * scale
+            edge = (one_row == k) | (one_row == k + 1)
+            r0_re = jnp.where(edge, jnp.where(one_row == k, 1.0, 0.0), re[k : k + 1])
+            r1_re = jnp.where(edge, jnp.where(one_row == k, 0.0, 1.0), re[k + 1 : k + 2])
+            r0_im = jnp.where(edge, 0.0, im[k : k + 1])
+            r1_im = jnp.where(edge, 0.0, im[k + 1 : k + 2])
+            t0_re = c * r0_re - (b_re * r1_re - b_im * r1_im)
+            t0_im = c * r0_im - (b_re * r1_im + b_im * r1_re)
+            t1_re = a * r1_re - (b_re * r0_re + b_im * r0_im)
+            t1_im = a * r1_im - (b_re * r0_im - b_im * r0_re)
+            next_re = jnp.where(pair, 0.0, re) - (c0_re * t0_re - c0_im * t0_im) - (c1_re * t1_re - c1_im * t1_im)
+            next_im = jnp.where(pair, 0.0, im) - (c0_re * t0_im + c0_im * t0_re) - (c1_re * t1_im + c1_im * t1_re)
             blocks[i] = (
-                jnp.where(rows == k, row_re, next_re),
-                jnp.where(rows == k, row_im, next_im),
+                jnp.where(rows == k, t0_re, jnp.where(rows == k + 1, t1_re, next_re)),
+                jnp.where(rows == k, t0_im, jnp.where(rows == k + 1, t1_im, next_im)),
             )
     return blocks
 

time: 38 us -> 34.2 us (0.900)
  Pallas kernels: 35.2 us -> 31.3 us
    pallas_call x1, Pallas kernels: 23.3 us -> 19.5 us  [few_snapshots(): pl.pallas_call(functools.partial(image_kernel, per_device, total_bins), o...]
where the time goes in v5:
time: 34.2 us; the launch traced here: 34.1 us
  Pallas kernels  31.3 us (92%)
  local copies, waits for them, and re-layouts  2.66 us (8%)
    pallas_call x1, Pallas kernels, few_snapshots(): pl.pallas_call(functools.partial(image_kernel, per_device, total_bins), o...  19.5 us
    pallas_call x1, Pallas kernels, few_snapshots(): pl.pallas_call(functools.partial(exchange_kernel, devices, per_device), o...  11.9 us
    unnamed x10, local copies, waits for them, and re-layouts  2.66 us

profile of v5, /device:TPU:0, one launch (start us, length us, event | category | flops | bytes accessed | tf_op | source)
XLA Modules:
  0.0 34.1 jit_solution(133244543518227285)
XLA Ops:
  0.0 0.0 copy-start
  0.0 1.2 %copy.6 = bf16[8,32,2,256]{3,0,2,1:T(8,128)(2,1)S(1)} copy(bf16[8,32,2,256]{3,2,1,0:T(2,128)(2,1)} %param.5) | data formatting | bytes 524288 | tf_op args[0]
  1.2 0.0 copy-start.1
  1.2 0.6 %copy-done.1 = s32[32]{0:T(128)S(1)} copy-done((s32[32]{0:T(128)S(1)}, s32[32]{0:T(128)}, u32[]{:S(2)}) %copy-start.1) | copy-done | bytes 152
  1.9 0.0 copy-start.3
  1.9 11.9 %shard_map.55 = bf16[16,16,512]{2,1,0:T(8,128)(2,1)S(1)} custom-call(s32[32]{0:T(128)S(1)} %copy-done.1, bf16[32,8,512]{2,1,0:T(8,128)(2,1)S(1)} %bitcast.6), custom_call_target="tpu_custom_call" | custom-call | tf_op jit(solution)/shard_map/pallas_call | solution.py:226
  13.8 0.0 copy-done.3
  13.8 0.1 copy.7
  13.9 0.0 copy-start.2
  13.9 0.0 copy-done
  14.0 0.6 %copy-done.2 = s32[32]{0:T(128)S(1)} copy-done((s32[32]{0:T(128)S(1)}, s32[32]{0:T(128)}, u32[]{:S(2)}) %copy-start.2) | copy-done | bytes 152
  14.6 19.5 %shard_map.56 = f32[2,2048]{1,0:T(2,128)} custom-call(s32[32]{0:T(128)S(1)} %copy-done.1, s32[32]{0:T(128)S(1)} %copy-done.2, bf16[256,512]{1,0:T(8,128)(2,1)S(1)} %bitcast.5, f32[32,2,2048]{2,1,0:T(2,128)S(1)} %copy-done, f32[256,2]{1,0:T(8,128)S(1)} %bitcast.7), custom_call_target="tpu_custom_call" | custom-call | tf_op jit(solution)/shard_map/pallas_call | solution.py:243
Async XLA Ops:
  0.0 13.9 %copy-start = (f32[32,2,2048]{2,1,0:T(2,128)S(1)}, f32[32,2,2048]{2,1,0:T(2,128)}, u32[]{:S(2)}) copy-start(f32[32,2,2048]{2,1,0:T(2,128)} %directions_ref.1) | copy-start | bytes 1572868
  1.2 0.7 %copy-start.1 = (s32[32]{0:T(128)S(1)}, s32[32]{0:T(128)}, u32[]{:S(2)}) copy-start(s32[32]{0:T(128)} %order_ref.3) | copy-start | bytes 388
  1.9 11.9 %copy-start.3 = (f32[2,256]{1,0:T(2,128)S(1)}, f32[2,256]{1,0:T(2,128)}, u32[]{:S(2)}) copy-start(f32[2,256]{1,0:T(2,128)} %param.7) | copy-start | bytes 6148
  13.9 0.7 %copy-start.2 = (s32[32]{0:T(128)S(1)}, s32[32]{0:T(128)}, u32[]{:S(2)}) copy-start(s32[32]{0:T(128)} %counts_ref.1) | copy-start | bytes 388

commit v6 on v5

--- a/solution.py
+++ b/solution.py
@@ -39,37 +39,33 @@
 
 def invert_small(blocks):
     n = blocks[0][0].shape[0]
-    rows = lax.broadcasted_iota(jnp.int32, (n, n), 0)
-    cols = lax.broadcasted_iota(jnp.int32, (n, n), 1)
-    one_row = lax.broadcasted_iota(jnp.int32, (1, n), 1)
-    blocks = list(blocks)
+    rows = lax.broadcasted_iota(jnp.int32, (n, 2 * n), 0)
+    cols = lax.broadcasted_iota(jnp.int32, (n, 2 * n), 1) % n
+    lane = lax.broadcasted_iota(jnp.int32, (1, 2 * n), 1)
+    packed = [jnp.concatenate([re, im], 1) for re, im in blocks]
     for k in range(0, n, 2):
         pair = (cols == k) | (cols == k + 1)
-        for i, (re, im) in enumerate(blocks):
-            c0_re = jnp.broadcast_to(re[:, k : k + 1], (n, n))
-            c0_im = jnp.broadcast_to(im[:, k : k + 1], (n, n))
-            c1_re = jnp.broadcast_to(re[:, k + 1 : k + 2], (n, n))
-            c1_im = jnp.broadcast_to(im[:, k + 1 : k + 2], (n, n))
+        edge = pair[:1]
+        for i, both in enumerate(packed):
+            c0_re = jnp.broadcast_to(both[:, k : k + 1], (n, 2 * n))
+            c0_im = jnp.broadcast_to(both[:, n + k : n + k + 1], (n, 2 * n))
+            c1_re = jnp.broadcast_to(both[:, k + 1 : k + 2], (n, 2 * n))
+            c1_im = jnp.broadcast_to(both[:, n + k + 1 : n + k + 2], (n, 2 * n))
             a, c = c0_re[k : k + 1], c1_re[k + 1 : k + 2]
             b_re, b_im = c1_re[k : k + 1], c1_im[k : k + 1]
             scale = 1.0 / (a * c - (b_re * b_re + b_im * b_im))
             a, c, b_re, b_im = a * scale, c * scale, b_re * scale, b_im * scale
-            edge = (one_row == k) | (one_row == k + 1)
-            r0_re = jnp.where(edge, jnp.where(one_row == k, 1.0, 0.0), re[k : k + 1])
-            r1_re = jnp.where(edge, jnp.where(one_row == k, 0.0, 1.0), re[k + 1 : k + 2])
-            r0_im = jnp.where(edge, 0.0, im[k : k + 1])
-            r1_im = jnp.where(edge, 0.0, im[k + 1 : k + 2])
-            t0_re = c * r0_re - (b_re * r1_re - b_im * r1_im)
-            t0_im = c * r0_im - (b_re * r1_im + b_im * r1_re)
-            t1_re = a * r1_re - (b_re * r0_re + b_im * r0_im)
-            t1_im = a * r1_im - (b_re * r0_im - b_im * r0_re)
-            next_re = jnp.where(pair, 0.0, re) - (c0_re * t0_re - c0_im * t0_im) - (c1_re * t1_re - c1_im * t1_im)
-            next_im = jnp.where(pair, 0.0, im) - (c0_re * t0_im + c0_im * t0_re) - (c1_re * t1_im + c1_im * t1_re)
-            blocks[i] = (
-                jnp.where(rows == k, t0_re, jnp.where(rows == k + 1, t1_re, next_re)),
-                jnp.where(rows == k, t0_im, jnp.where(rows == k + 1, t1_im, next_im)),
-            )
-    return blocks
+            r0 = jnp.where(edge, jnp.where(lane == k, 1.0, 0.0), both[k : k + 1])
+            r1 = jnp.where(edge, jnp.where(lane == k + 1, 1.0, 0.0), both[k + 1 : k + 2])
+            i0 = jnp.concatenate([-r0[:, n:], r0[:, :n]], 1)
+            i1 = jnp.concatenate([-r1[:, n:], r1[:, :n]], 1)
+            t0 = c * r0 - (b_re * r1 + b_im * i1)
+            u0 = c * i0 - (b_re * i1 - b_im * r1)
+            t1 = a * r1 - (b_re * r0 - b_im * i0)
+            u1 = a * i1 - (b_re * i0 + b_im * r0)
+            rest = jnp.where(pair, 0.0, both) - (c0_re * t0 + c0_im * u0) - (c1_re * t1 + c1_im * u1)
+            packed[i] = jnp.where(rows == k, t0, jnp.where(rows == k + 1, t1, rest))
+    return [(both[:, :n], both[:, n:]) for both in packed]
 
 
 def put_rows(whole, rows, start):

time: 34.2 us -> 34.9 us (1.020)
  Pallas kernels: 31.3 us -> 32.1 us
    pallas_call x1, Pallas kernels: 19.5 us -> 20.2 us  [few_snapshots(): pl.pallas_call(functools.partial(image_kernel, per_device, total_bins), o...]
where the time goes in v6:
time: 34.9 us; the launch traced here: 34.8 us
  Pallas kernels  32.1 us (92%)
  local copies, waits for them, and re-layouts  2.66 us (8%)
    pallas_call x1, Pallas kernels, few_snapshots(): pl.pallas_call(functools.partial(image_kernel, per_device, total_bins), o...  20.2 us
    pallas_call x1, Pallas kernels, few_snapshots(): pl.pallas_call(functools.partial(exchange_kernel, devices, per_device), o...  11.9 us
    unnamed x10, local copies, waits for them, and re-layouts  2.66 us

profile of v6, /device:TPU:0, one launch (start us, length us, event | category | flops | bytes accessed | tf_op | source)
XLA Modules:
  0.0 34.8 jit_solution(15066124983942452363)
XLA Ops:
  0.0 0.0 copy-start
  0.0 1.2 %copy.6 = bf16[8,32,2,256]{3,0,2,1:T(8,128)(2,1)S(1)} copy(bf16[8,32,2,256]{3,2,1,0:T(2,128)(2,1)} %param.5) | data formatting | bytes 524288 | tf_op args[0]
  1.2 0.0 copy-start.1
  1.2 0.6 %copy-done.1 = s32[32]{0:T(128)S(1)} copy-done((s32[32]{0:T(128)S(1)}, s32[32]{0:T(128)}, u32[]{:S(2)}) %copy-start.1) | copy-done | bytes 152
  1.9 0.0 copy-start.3
  1.9 11.9 %shard_map.55 = bf16[16,16,512]{2,1,0:T(8,128)(2,1)S(1)} custom-call(s32[32]{0:T(128)S(1)} %copy-done.1, bf16[32,8,512]{2,1,0:T(8,128)(2,1)S(1)} %bitcast.6), custom_call_target="tpu_custom_call" | custom-call | tf_op jit(solution)/shard_map/pallas_call | solution.py:222
  13.8 0.0 copy-done.3
  13.8 0.1 copy.7
  13.9 0.0 copy-start.2
  13.9 0.0 copy-done
  14.0 0.6 %copy-done.2 = s32[32]{0:T(128)S(1)} copy-done((s32[32]{0:T(128)S(1)}, s32[32]{0:T(128)}, u32[]{:S(2)}) %copy-start.2) | copy-done | bytes 152
  14.6 20.2 %shard_map.56 = f32[2,2048]{1,0:T(2,128)} custom-call(s32[32]{0:T(128)S(1)} %copy-done.1, s32[32]{0:T(128)S(1)} %copy-done.2, bf16[256,512]{1,0:T(8,128)(2,1)S(1)} %bitcast.5, f32[32,2,2048]{2,1,0:T(2,128)S(1)} %copy-done, f32[256,2]{1,0:T(8,128)S(1)} %bitcast.7), custom_call_target="tpu_custom_call" | custom-call | tf_op jit(solution)/shard_map/pallas_call | solution.py:239
Async XLA Ops:
  0.0 13.9 %copy-start = (f32[32,2,2048]{2,1,0:T(2,128)S(1)}, f32[32,2,2048]{2,1,0:T(2,128)}, u32[]{:S(2)}) copy-start(f32[32,2,2048]{2,1,0:T(2,128)} %directions_ref.1) | copy-start | bytes 1572868
  1.2 0.7 %copy-start.1 = (s32[32]{0:T(128)S(1)}, s32[32]{0:T(128)}, u32[]{:S(2)}) copy-start(s32[32]{0:T(128)} %order_ref.3) | copy-start | bytes 388
  1.9 11.9 %copy-start.3 = (f32[2,256]{1,0:T(2,128)S(1)}, f32[2,256]{1,0:T(2,128)}, u32[]{:S(2)}) copy-start(f32[2,256]{1,0:T(2,128)} %param.7) | copy-start | bytes 6148
  13.9 0.7 %copy-start.2 = (s32[32]{0:T(128)S(1)}, s32[32]{0:T(128)}, u32[]{:S(2)}) copy-start(s32[32]{0:T(128)} %counts_ref.1) | copy-start | bytes 388

commit v7 on v5

--- a/solution.py
+++ b/solution.py
@@ -113,8 +113,14 @@
 
 
 def image_kernel(per_device, total_bins, order_ref, counts_ref, snaps_ref, directions_ref, spots_ref, out_ref,
-                 solver_ref, turned_ref, spot_ref):
+                 solver_ref, turned_ref, spot_ref, angles_ref, angles_sem):
     first = lax.axis_index("bins") * per_device
+    fetches = [
+        pltpu.make_async_copy(directions_ref.at[order_ref[first + local]], angles_ref.at[local], angles_sem.at[local])
+        for local in range(per_device)
+    ]
+    for fetch in fetches:
+        fetch.start()
     snap = snaps_ref.shape[0] // per_device
     sensors = spots_ref.shape[0]
     looks = out_ref.shape[1]
@@ -142,6 +148,8 @@
         solver_ref[local, 0] = high
         solver_ref[local, 1] = low
     out_ref[...] = jnp.zeros_like(out_ref)
+    for fetch in fetches:
+        fetch.wait()
     for local in range(per_device):
         bin_id = order_ref[first + local]
         count = counts_ref[bin_id]
@@ -151,7 +159,7 @@
 
         def one_block(block, carry):
             offset = pl.multiple_of(block * WIDE, WIDE)
-            piece = directions_ref[bin_id, :, pl.ds(offset, WIDE)]
+            piece = angles_ref[local, :, pl.ds(offset, WIDE)]
             x = jnp.concatenate([spot_ref[0]] * (WIDE // 128), 1)
             y = jnp.concatenate([spot_ref[1]] * (WIDE // 128), 1)
             turns = x * piece[0:1] + y * piece[1:2]
@@ -243,12 +251,14 @@
     return pl.pallas_call(
         functools.partial(image_kernel, per_device, total_bins),
         out_shape=jax.ShapeDtypeStruct((per_device, looks), F32),
-        in_specs=[smem, smem, vmem, vmem, vmem],
+        in_specs=[smem, smem, vmem, pl.BlockSpec(memory_space=pl.ANY), vmem],
         out_specs=vmem,
         scratch_shapes=[
             pltpu.VMEM((per_device, 2, 2 * snap, 2 * sensors), BF16),
             pltpu.VMEM((per_device, 2 * sensors, 2 * snap), BF16),
             pltpu.VMEM((2, sensors, 128), F32),
+            pltpu.VMEM((per_device, 2, looks), F32),
+            pltpu.SemaphoreType.DMA((per_device,)),
         ],
         compiler_params=pltpu.CompilerParams(vmem_limit_bytes=40 * 1024 * 1024),
     )(bin_order, look_counts, arrived, directions, positions.T)

time: 34.2 us -> 34.5 us (level)
  Pallas kernels: 31.3 us -> 31.7 us
where the time goes in v7:
time: 34.5 us; the launch traced here: 34.4 us
  Pallas kernels  31.7 us (92%)
  local copies, waits for them, and re-layouts  2.66 us (8%)
    pallas_call x1, Pallas kernels, few_snapshots(): pl.pallas_call(functools.partial(image_kernel, per_device, total_bins), o...  19.8 us
    pallas_call x1, Pallas kernels, few_snapshots(): pl.pallas_call(functools.partial(exchange_kernel, devices, per_device), o...  11.9 us
    unnamed x10, local copies, waits for them, and re-layouts  2.66 us

profile of v7, /device:TPU:0, one launch (start us, length us, event | category | flops | bytes accessed | tf_op | source)
XLA Modules:
  0.0 34.4 jit_solution(5577874927744294155)
XLA Ops:
  0.0 0.0 copy-start
  0.0 1.2 %copy.6 = bf16[8,32,2,256]{3,0,2,1:T(8,128)(2,1)S(1)} copy(bf16[8,32,2,256]{3,2,1,0:T(2,128)(2,1)} %param.5) | data formatting | bytes 524288 | tf_op args[0]
  1.2 0.0 copy-start.1
  1.2 0.6 %copy-done.1 = s32[32]{0:T(128)S(1)} copy-done((s32[32]{0:T(128)S(1)}, s32[32]{0:T(128)}, u32[]{:S(2)}) %copy-start.1) | copy-done | bytes 152
  1.9 0.0 copy-start.3
  1.9 11.9 %shard_map.55 = bf16[16,16,512]{2,1,0:T(8,128)(2,1)S(1)} custom-call(s32[32]{0:T(128)S(1)} %copy-done.1, bf16[32,8,512]{2,1,0:T(8,128)(2,1)S(1)} %bitcast.6), custom_call_target="tpu_custom_call" | custom-call | tf_op jit(solution)/shard_map/pallas_call | solution.py:234
  13.8 0.0 copy-done.3
  13.8 0.1 copy.7
  13.9 0.0 copy-start.2
  13.9 0.0 copy-done
  14.0 0.6 %copy-done.2 = s32[32]{0:T(128)S(1)} copy-done((s32[32]{0:T(128)S(1)}, s32[32]{0:T(128)}, u32[]{:S(2)}) %copy-start.2) | copy-done | bytes 152
  14.6 19.8 %shard_map.56 = f32[2,2048]{1,0:T(2,128)} custom-call(s32[32]{0:T(128)S(1)} %copy-done.1, s32[32]{0:T(128)S(1)} %copy-done.2, bf16[256,512]{1,0:T(8,128)(2,1)S(1)} %bitcast.5, f32[32,2,2048]{2,1,0:T(2,128)S(1)} %copy-done, f32[256,2]{1,0:T(8,128)S(1)} %bitcast.7), custom_call_target="tpu_custom_call" | custom-call | tf_op jit(solution)/shard_map/pallas_call | solution.py:251
Async XLA Ops:
  0.0 13.9 %copy-start = (f32[32,2,2048]{2,1,0:T(2,128)S(1)}, f32[32,2,2048]{2,1,0:T(2,128)}, u32[]{:S(2)}) copy-start(f32[32,2,2048]{2,1,0:T(2,128)} %directions_ref.1) | copy-start | bytes 1572868
  1.2 0.7 %copy-start.1 = (s32[32]{0:T(128)S(1)}, s32[32]{0:T(128)}, u32[]{:S(2)}) copy-start(s32[32]{0:T(128)} %order_ref.3) | copy-start | bytes 388
  1.9 11.9 %copy-start.3 = (f32[2,256]{1,0:T(2,128)S(1)}, f32[2,256]{1,0:T(2,128)}, u32[]{:S(2)}) copy-start(f32[2,256]{1,0:T(2,128)} %param.7) | copy-start | bytes 6148
  13.9 0.7 %copy-start.2 = (s32[32]{0:T(128)S(1)}, s32[32]{0:T(128)}, u32[]{:S(2)}) copy-start(s32[32]{0:T(128)} %counts_ref.1) | copy-start | bytes 388
